TPU v7x, 512 devices: a whole 4x4x16 slice. The times are simulated.
512 devices in a mesh: frames: 64 (over z, y_hi, core), mp: 4 (over x), dp: 2 (over y_lo).
Axes of the slice: x: 4, y: 4 (y_hi: 2, y_lo: 2; y = y_hi * 2 + y_lo), z: 16, core: 2. Of those that a mesh axis runs over, the one named last changes fastest.
Arguments:
- projections: bfloat16 [2, 128, 96, 3, 3584], P('dp', 'frames', None, None, 'mp'), may hold values from -18 to 18
- perturbation: bfloat16 [2, 128, 96, 3, 3584], P('dp', 'frames', None, None, 'mp'), may hold values from -44 to 44
- out_weight: bfloat16 [3584, 3584], P('frames', 'mp'), may hold values from -0.09375 to 0.09375
- norm_gain: float32 [3584], P('mp'), may hold values from 0.25 to 1.75
- live_counts: int32 [2, 128], P('dp'), may hold values from 72 to 96, as said below
Outputs:
- features: bfloat16 [2, 128, 96, 3584], P('dp', 'frames', None, 'mp')
- penalty: float32 [2], P('dp')
- gain_grad: float32 [3584], P('mp')
Inputs may be any that keep to these rules, and one draw needn't show every extreme that they name: `live_counts`: in each clip one slot has all 96 tokens live and another has 72 live.
All inputs are finite; a program needn't handle non-finite values.
Results may differ from a plain program's by a relative error of at most 0.0057.
Values may be sent and summed in bfloat16 or wider, within the bound.
A program may use at most 64 MiB of HBM per device.

v0:
```python
import math
import jax
import jax.numpy as jnp
from jax import lax
from jax.sharding import PartitionSpec as P

HEAD_DIM = 128
sigma_noise = 0.25
epsilon = 1e-06


def padded(cells, sides, width):
    for axis, dim in sides:
        count = lax.axis_size(axis)
        ends = count - 1
        head = lax.slice_in_dim(cells, 0, width, axis=dim)
        tail = lax.slice_in_dim(cells, cells.shape[dim] - width, cells.shape[dim], axis=dim)
        cells = jnp.concatenate(
            [
                lax.ppermute(tail, axis, [(i, (i + 1) % count) for i in range(ends)]),
                cells,
                lax.ppermute(head, axis, [((i + 1) % count, i) for i in range(ends)]),
            ],
            axis=dim,
        )
    return cells


def split_heads(tensor):
    return tensor.reshape(tensor.shape[:-1] + (tensor.shape[-1] // HEAD_DIM, HEAD_DIM))


def attend(query_rows, key_rows, value_rows, key_live):
    scores = jnp.einsum(
        "wrhe,wmhe->whrm",
        split_heads(query_rows),
        split_heads(key_rows),
        preferred_element_type=jnp.float32,
    ) * (1.0 / math.sqrt(HEAD_DIM))
    live_float = key_live[:, None, None, :]
    masked = jnp.where(live_float, scores, -1e30)
    largest = jnp.max(masked, axis=-1, keepdims=True)
    weights = jnp.exp(masked - largest) * live_float.astype(jnp.float32)
    probabilities = (weights / jnp.sum(weights, axis=-1, keepdims=True)).astype(jnp.bfloat16)
    mixed = jnp.einsum(
        "whrm,wmhe->wrhe",
        probabilities,
        split_heads(value_rows),
        preferred_element_type=jnp.float32,
    )
    return mixed.astype(jnp.bfloat16).reshape(query_rows.shape)


def attend_each(query_rows, key_rows, value_rows, key_live):

    def one_window(item):
        return attend(item[0][None], item[1][None], item[2][None], item[3][None])[0]

    return lax.map(one_window, (query_rows, key_rows, value_rows, key_live))


def local(projections, perturbation, out_weight, norm_gain, live_counts):
    tile_len = projections.shape[2]
    local_width = projections.shape[4]
    slab_count = lax.axis_size("frames")
    slab_index = lax.axis_index("frames")
    model_width = local_width * lax.axis_size("mp")
    token_total = projections.shape[1] * slab_count * tile_len
    perturbed = (
        projections.astype(jnp.float32) + sigma_noise * perturbation.astype(jnp.float32)
    ).astype(jnp.bfloat16)
    streams = jnp.concatenate([projections, perturbed], axis=0)
    padded_counts = jnp.pad(live_counts[0], (1, 1))
    nearby = lax.dynamic_slice_in_dim(padded_counts, 2 * slab_index, 4)
    token_pos = jnp.arange(tile_len)
    live_near = token_pos[None, :] < nearby[:, None]
    key_values = streams[:, :, :, 1:, :]
    widened = padded(key_values, (("frames", 1),), 1)
    grouped = widened.reshape(4, 2 * tile_len, 2, local_width)
    query_rows = streams[:, :, :, 0, :].reshape(4, tile_len, local_width)
    key_live = jnp.tile(live_near.reshape(2, 2 * tile_len), (2, 1))
    attended = attend_each(query_rows, grouped[:, :, 0], grouped[:, :, 1], key_live)
    attended = attended.reshape(2, 2, tile_len, local_width)
    gathered = lax.all_gather(attended, "mp", axis=3, tiled=True)
    flat_rows = gathered.reshape(-1, model_width)
    projected = jnp.dot(
        flat_rows,
        lax.all_gather(out_weight, "frames", axis=0, tiled=True),
        preferred_element_type=jnp.float32,
    )
    projected = projected.reshape(2, 2, tile_len, local_width)
    squares = lax.psum(jnp.sum(projected * projected, axis=-1), "mp")
    normed = projected * lax.rsqrt(squares / model_width + epsilon)[..., None]
    own_live = live_near[1:3].astype(jnp.float32)[:, :, None]
    features = (normed[0] * norm_gain * own_live).astype(jnp.bfloat16)[None]
    difference = (normed[1] - normed[0]) * own_live
    feature_sums = jnp.sum(difference * difference, axis=(0, 1))
    local_penalty = jnp.sum(feature_sums * norm_gain * norm_gain).reshape(1)
    penalty = lax.psum(local_penalty, ("frames", "mp")) / (
        sigma_noise * sigma_noise * token_total * model_width
    )
    gain_grad = (
        norm_gain
        * lax.psum(feature_sums, ("frames", "dp"))
        / (sigma_noise * sigma_noise * token_total)
    )
    return (features, penalty, gain_grad)


def solution(mesh):
    placed = (
        P("dp", "frames", None, None, "mp"),
        P("dp", "frames", None, None, "mp"),
        P("frames", "mp"),
        P("mp"),
        P("dp", None),
    )
    return jax.shard_map(
        local,
        mesh=mesh,
        in_specs=placed,
        out_specs=(P("dp", "frames", None, "mp"), P("dp"), P("mp")),
        check_vma=False,
    )
```

profile of v0, /device:TPU:2, one launch (start us, length us, event | category | flops | bytes accessed | tf_op | source)
XLA Modules:
  0.0 1192.0 jit_solution(10483000948008665854)
XLA Ops:
  7.2 1.9 add_convert_fusion
  9.2 1.2 fusion.25
  10.4 2.6 collective-permute-start
  13.0 1.3 collective-permute-start.1
  15.0 4.5 collective-permute-done.1
  19.5 1.7 pad_maximum_fusion
  21.5 1.3 slice_bitcast_fusion
  22.8 22.9 %while.10 = (s32[]{:T(128)}, bf16[4,96,896]{2,1,0:T(8,128)(2,1)}, bf16[4,192,896]{2,1,0:T(8,128)(2,1)}, pred[4,192]{1,0:T(4,128)(4,1)S(1)}, bf16[4,96,896]{2,1,0...) while((s32[]{:T(128)}, bf16[4,96,896]{2,1,0:T(8,128)(2,1)}, bf16[4,192,896]{2,1,0:T(8,128)(2,1)}, ...), condition=%wide.region_3.4_spmd, body=%wide.region_0.3_spmd.sunk | while | flops 67049856 | bytes 5857369 | solution.py:59
  22.8 1.0 constant_dynamic-slice_fusion.5
  24.5 1.5 fusion.45
  26.4 1.4 fusion.46
  27.8 0.7 bitcast_dynamic-update-slice_fusion.2
  28.5 1.0 constant_dynamic-slice_fusion.5
  30.2 1.5 fusion.45
  32.1 1.4 fusion.46
  34.2 1.0 constant_dynamic-slice_fusion.5
  36.0 1.5 fusion.45
  37.9 1.4 fusion.46
  39.3 0.7 bitcast_dynamic-update-slice_fusion.2
  40.0 1.0 constant_dynamic-slice_fusion.5
  41.7 1.5 fusion.45
  43.6 1.4 fusion.46
  45.0 0.7 bitcast_dynamic-update-slice_fusion.2
  45.8 0.7 all-gather.5.cloned.1.call-update
  46.5 59.2 %all-gather.3.cloned.1.call-done = bf16[2,2,96,3584]{3,2,1,0:T(8,128)(2,1)} async-done(((bf16[2,2,96,896]{3,2,1,0:T(8,128)(2,1)}), bf16[2,2,96,3584]{3,2,1,0:T(8,128)(2,1)}) %all-gather.3.cloned.1.call-update) | async-done | bytes 2752528 | tf_op jit(solution)/shard_map/all_gather | solution.py:84
  105.8 162.8 %all-gather.5.cloned.1.call-done = bf16[3584,896]{1,0:T(8,128)(2,1)} async-done(((bf16[56,896]{1,0:T(8,128)(2,1)}), bf16[3584,896]{1,0:T(8,128)(2,1)}) %all-gather.5.cloned.1.call-update) | async-done | bytes 6422544 | tf_op jit(solution)/shard_map/all_gather | solution.py:88
  268.6 6.7 multiply_reduce_fusion
  275.3 8.6 psum.21
  284.3 247.6 %psum.23 = f32[896]{0:T(1024)S(1)} all-reduce(f32[896]{0:T(1024)S(1)} %fusion.29), channel_id=1, replica_groups=mesh['frames'=64,'mp'=4,'dp'=2] {'frames','dp'}, use_global_device_ids=true, to_apply=%region_9.10 | all-reduce | flops 896 | bytes 7168 | tf_op jit(solution)/shard_map/psum | solution.py:104
  532.0 0.8 multiply_convert_fusion
  532.8 1.2 multiply_multiply_fusion.1
  534.0 649.4 %psum.22 = f32[1]{0:T(128)} all-reduce(f32[1]{0:T(128)} %bitcast.11), channel_id=1, replica_groups=mesh['frames'=64,'mp'=4,'dp'=2] {'frames','mp'}, use_global_device_ids=true, to_apply=%region_8.9 | all-reduce | flops 1 | bytes 8 | tf_op jit(solution)/shard_map/psum | solution.py:99
  (53 shorter events, 6.5 us)
Async XLA Ops:
  7.2 2.0 copy-start
  7.2 98.6 %all-gather.3.cloned.1.call-start = ((), (), s32[]{:S(2)}) async-start(), calls=%async_computation | async-start | bytes 3440640 | tf_op jit(solution)/shard_map/all_gather | solution.py:84
  9.2 5.1 copy-start.2
  10.4 4.6 collective-permute-start
  13.0 6.5 collective-permute-start.1
  45.7 222.9 %all-gather.5.cloned.1.call-start = ((), (), s32[]{:S(2)}) async-start(), calls=%async_computation.1 | async-start | bytes 6522880 | tf_op jit(solution)/shard_map/all_gather | solution.py:88
  283.9 248.0 %copy-start.1 = (f32[896]{0:T(1024)S(1)}, f32[896]{0:T(1024)}, u32[]{:S(2)}) copy-start(f32[896]{0:T(1024)} %param.10) | copy-start | bytes 10756
Sparse Core Ops, SparseCore 0:
  45.8 59.8 all-gather.2
  109.0 159.5 all-gather.4
where the time goes:
time: 1190 us
  blocking collectives  906 us (76%)
  waiting for transfers between devices  227 us (19%)
  matrix products  18.3 us (2%)
  between operations  15.9 us (1%)
  local copies, waits for them, and re-layouts  13.2 us (1%)
    psum x1, blocking collectives, local(): lax.psum(local_penalty, ('frames', 'mp'))  649 us
    psum x1, blocking collectives, local(): lax.psum(feature_sums, ('frames', 'dp'))  248 us
    all_gather x1, waiting for transfers between devices, local(): lax.all_gather(out_weight, 'frames', axis=0, tiled=True)  163 us
    all_gather x1, waiting for transfers between devices, local(): gathered = lax.all_gather(attended, 'mp', axis=3, tiled=True)  59.2 us
  transfers between devices with their start and end apart: 4, of which 3 were waited for; matrix products, arithmetic and copies ran while one was open for 0% of the time, Pallas kernels for 0%

commit v1 on v0

--- a/solution.py
+++ b/solution.py
@@ -7,6 +7,11 @@
 HEAD_DIM = 128
 sigma_noise = 0.25
 epsilon = 1e-06
+
+
+def one_after_other(value, inner_axis, outer_axis):
+    partial = lax.psum(value, inner_axis)
+    return lax.psum(partial, outer_axis)
 
 
 def padded(cells, sides, width):
@@ -96,7 +101,7 @@
     difference = (normed[1] - normed[0]) * own_live
     feature_sums = jnp.sum(difference * difference, axis=(0, 1))
     local_penalty = jnp.sum(feature_sums * norm_gain * norm_gain).reshape(1)
-    penalty = lax.psum(local_penalty, ("frames", "mp")) / (
+    penalty = one_after_other(local_penalty, "mp", "frames") / (
         sigma_noise * sigma_noise * token_total * model_width
     )
     gain_grad = (

time: 1190 us -> 684 us (0.57)
  the two profiles are of different devices: /device:TPU:2 before, /device:TPU:1 now
where the time goes in v1:
time: 684 us; the launch traced here: 683 us
  blocking collectives  395 us (58%)
  waiting for transfers between devices  221 us (32%)
  matrix products  18.3 us (3%)
  between operations  15.9 us (2%)
  local copies, waits for them, and re-layouts  13.2 us (2%)
  starting transfers between devices  11 us (2%)
  other arithmetic  7.59 us (1%)
    psum x1, blocking collectives, local(): lax.psum(feature_sums, ('frames', 'dp'))  247 us
    all_gather x1, waiting for transfers between devices, local(): lax.all_gather(out_weight, 'frames', axis=0, tiled=True)  162 us
    psum x1, blocking collectives, one_after_other(): return lax.psum(partial, outer_axis)  133 us
    all_gather x1, waiting for transfers between devices, local(): gathered = lax.all_gather(attended, 'mp', axis=3, tiled=True)  48.2 us
  transfers between devices with their start and end apart: 4, of which 3 were waited for; matrix products, arithmetic and copies ran while one was open for 0% of the time, Pallas kernels for 0%

profile of v1, /device:TPU:1, one launch (start us, length us, event | category | flops | bytes accessed | tf_op | source)
XLA Modules:
  0.0 683.1 jit_solution(6552076949508623243)
XLA Ops:
  7.2 1.9 add_convert_fusion
  9.2 1.2 fusion.25
  10.4 6.2 collective-permute-start
  16.6 4.7 collective-permute-start.1
  22.0 10.1 %collective-permute-done = bf16[2,1,96,2,896]{4,2,3,1,0:T(8,128)(2,1)} collective-permute-done((bf16[2,1,96,2,896]{4,2,3,1,0:T(8,128)(2,1)}, bf16[2,1,96,2,896]{4,2,3,1,0:T(8,128)(2,1)}, u32[]{:S(2)}, u32[]{:S(2)}) %collective-permute-start) | collective-permute-done | bytes 688160 | tf_op jit(solution)/shard_map/ppermute | solution.py:25
  32.2 1.7 pad_maximum_fusion
  34.1 1.3 slice_bitcast_fusion
  35.4 22.9 %while.10 = (s32[]{:T(128)}, bf16[4,96,896]{2,1,0:T(8,128)(2,1)}, bf16[4,192,896]{2,1,0:T(8,128)(2,1)}, pred[4,192]{1,0:T(4,128)(4,1)S(1)}, bf16[4,96,896]{2,1,0...) while((s32[]{:T(128)}, bf16[4,96,896]{2,1,0:T(8,128)(2,1)}, bf16[4,192,896]{2,1,0:T(8,128)(2,1)}, ...), condition=%wide.region_3.4_spmd, body=%wide.region_0.3_spmd.sunk | while | flops 67049856 | bytes 5857369 | solution.py:64
  35.4 1.0 constant_dynamic-slice_fusion.5
  37.2 1.5 fusion.45
  39.1 1.4 fusion.46
  40.5 0.7 bitcast_dynamic-update-slice_fusion.2
  41.2 1.0 constant_dynamic-slice_fusion.5
  42.9 1.5 fusion.45
  44.8 1.4 fusion.46
  46.9 1.0 constant_dynamic-slice_fusion.5
  48.6 1.5 fusion.45
  50.5 1.4 fusion.46
  52.6 1.0 constant_dynamic-slice_fusion.5
  54.4 1.5 fusion.45
  56.3 1.4 fusion.46
  57.7 0.7 bitcast_dynamic-update-slice_fusion.2
  58.4 0.7 all-gather.5.cloned.1.call-update
  59.2 48.2 %all-gather.3.cloned.1.call-done = bf16[2,2,96,3584]{3,2,1,0:T(8,128)(2,1)} async-done(((bf16[2,2,96,896]{3,2,1,0:T(8,128)(2,1)}), bf16[2,2,96,3584]{3,2,1,0:T(8,128)(2,1)}) %all-gather.3.cloned.1.call-update) | async-done | bytes 2752528 | tf_op jit(solution)/shard_map/all_gather | solution.py:89
  107.5 162.4 %all-gather.5.cloned.1.call-done = bf16[3584,896]{1,0:T(8,128)(2,1)} async-done(((bf16[56,896]{1,0:T(8,128)(2,1)}), bf16[3584,896]{1,0:T(8,128)(2,1)}) %all-gather.5.cloned.1.call-update) | async-done | bytes 6422544 | tf_op jit(solution)/shard_map/all_gather | solution.py:93
  269.9 6.7 multiply_reduce_fusion
  276.6 8.4 %psum.28 = f32[2,2,96]{2,1,0:T(2,128)S(1)} all-reduce(f32[2,2,96]{2,1,0:T(2,128)S(1)} %get-tuple-element.58), channel_id=1, replica_groups=mesh['frames'=64,'mp'=4,'dp'=2] {'mp'}, use_global_device_ids=true, to_apply=%region_5.6 | all-reduce | flops 384 | bytes 3072 | tf_op jit(solution)/shard_map/psum | solution.py:97
  285.4 247.0 %psum.31 = f32[896]{0:T(1024)S(1)} all-reduce(f32[896]{0:T(1024)S(1)} %fusion.29), channel_id=1, replica_groups=mesh['frames'=64,'mp'=4,'dp'=2] {'frames','dp'}, use_global_device_ids=true, to_apply=%region_10.11 | all-reduce | flops 896 | bytes 7168 | tf_op jit(solution)/shard_map/psum | solution.py:109
  532.5 1.2 multiply_multiply_fusion.1
  533.7 6.6 psum.29
  540.3 0.8 multiply_convert_fusion
  541.1 133.3 %psum.30 = f32[1]{0:T(128)} all-reduce(f32[1]{0:T(128)} %psum.29), channel_id=1, replica_groups=mesh['frames'=64,'mp'=4,'dp'=2] {'frames'}, use_global_device_ids=true, to_apply=%region_9.10 | all-reduce | flops 1 | bytes 8 | tf_op jit(solution)/shard_map/psum | solution.py:14
  (54 shorter events, 7.2 us)
Async XLA Ops:
  7.2 2.0 copy-start
  7.2 100.3 %all-gather.3.cloned.1.call-start = ((), (), s32[]{:S(2)}) async-start(), calls=%async_computation | async-start | bytes 3440640 | tf_op jit(solution)/shard_map/all_gather | solution.py:89
  9.2 12.2 %copy-start.2 = (s32[1,128]{1,0:T(1,128)S(1)}, s32[1,128]{1,0:T(1,128)}, u32[]{:S(2)}) copy-start(s32[1,128]{1,0:T(1,128)} %param.11) | copy-start | bytes 1540
  10.4 21.8 %collective-permute-start = (bf16[2,1,96,2,896]{4,2,3,1,0:T(8,128)(2,1)}, bf16[2,1,96,2,896]{4,2,3,1,0:T(8,128)(2,1)}, u32[]{:S(2)}, u32[]{:S(2)}) collective-permute-start(bf16[2,1,96,2,896]{4,2,3,1,0:T(8,128)(2,1)} %get-tuple-element.54), channel_id=1, source_target_pairs={{0,8},{8,16},{16,24},{24,32},{32,40},{40,48},{48,56},{56,64},{64,7... | collective-permute-start | bytes 2064392 | tf_op jit(solution)/shard_map/ppermute | solution.py:25
  16.6 15.6 %collective-permute-start.1 = (bf16[2,1,96,2,896]{4,2,3,1,0:T(8,128)(2,1)}, bf16[2,1,96,2,896]{4,2,3,1,0:T(8,128)(2,1)}, u32[]{:S(2)}, u32[]{:S(2)}) collective-permute-start(bf16[2,1,96,2,896]{4,2,3,1,0:T(8,128)(2,1)} %get-tuple-element.55), channel_id=1, source_target_pairs={{8,0},{16,8},{24,16},{32,24},{40,32},{48,40},{56,48},{64,56},{72,6... | collective-permute-start | bytes 2064392 | tf_op jit(solution)/shard_map/ppermute | solution.py:27
  58.4 211.5 %all-gather.5.cloned.1.call-start = ((), (), s32[]{:S(2)}) async-start(), calls=%async_computation.1 | async-start | bytes 6522880 | tf_op jit(solution)/shard_map/all_gather | solution.py:93
  285.0 247.4 %copy-start.1 = (f32[896]{0:T(1024)S(1)}, f32[896]{0:T(1024)}, u32[]{:S(2)}) copy-start(f32[896]{0:T(1024)} %param.10) | copy-start | bytes 10756
Sparse Core Ops, SparseCore 0:
  58.5 48.9 all-gather.2
  110.6 159.1 all-gather.4

commit v2 on v0

--- a/solution.py
+++ b/solution.py
@@ -1,3 +1,4 @@
+import functools
 import math
 import jax
 import jax.numpy as jnp
@@ -7,6 +8,15 @@
 HEAD_DIM = 128
 sigma_noise = 0.25
 epsilon = 1e-06
+
+
+def thing_pass(vals, axis_tag, dim_at):
+    low = lax.all_to_all(jnp.stack([vals] * lax.axis_size(axis_tag), axis=0), axis_tag, 0, 0)
+    item_now = jnp.concatenate(low, axis=dim_at)
+    return item_now
+
+
+store_rows_by_axis = functools.partial(thing_pass, axis_tag="frames", dim_at=0)
 
 
 def padded(cells, sides, width):
@@ -84,9 +94,7 @@
     gathered = lax.all_gather(attended, "mp", axis=3, tiled=True)
     flat_rows = gathered.reshape(-1, model_width)
     projected = jnp.dot(
-        flat_rows,
-        lax.all_gather(out_weight, "frames", axis=0, tiled=True),
-        preferred_element_type=jnp.float32,
+        flat_rows, store_rows_by_axis(out_weight), preferred_element_type=jnp.float32
     )
     projected = projected.reshape(2, 2, tile_len, local_width)
     squares = lax.psum(jnp.sum(projected * projected, axis=-1), "mp")

time: 1190 us -> 1310 us (1.10)
  waiting for transfers between devices: 227 us -> 322 us
  starting transfers between devices: 3.95 us -> 23.1 us
    all_gather x1, waiting for transfers between devices: 59.2 us -> 317 us  [local(): gathered = lax.all_gather(attended, 'mp', axis=3, tiled=True)]
    all_gather x1 -> x0, waiting for transfers between devices: 163 us -> none  [local(): lax.all_gather(out_weight, 'frames', axis=0, tiled=True)]
    all_to_all x0 -> x1, starting transfers between devices: none -> 19.1 us  [thing_pass(): lax.all_to_all(jnp.stack([vals] * lax.axis_size(axis_tag), axis=0), axis_...]
  transfers between devices with their start and end apart: 4 -> 4, of which waited for: 3 -> 2; matrix products, arithmetic and copies ran while one was open for 0% -> 2% of each run, Pallas kernels for 0% -> 0%
where the time goes in v2:
time: 1310 us
  blocking collectives  908 us (69%)
  waiting for transfers between devices  322 us (25%)
  starting transfers between devices  23.1 us (2%)
  matrix products  18.1 us (1%)
  local copies, waits for them, and re-layouts  17.4 us (1%)
  between operations  15.9 us (1%)
    psum x1, blocking collectives, local(): lax.psum(local_penalty, ('frames', 'mp'))  648 us
    all_gather x1, waiting for transfers between devices, local(): gathered = lax.all_gather(attended, 'mp', axis=3, tiled=True)  317 us
    psum x1, blocking collectives, local(): lax.psum(feature_sums, ('frames', 'dp'))  250 us
  transfers between devices with their start and end apart: 4, of which 2 were waited for; matrix products, arithmetic and copies ran while one was open for 2% of the time, Pallas kernels for 0%

profile of v2, /device:TPU:2, one launch (start us, length us, event | category | flops | bytes accessed | tf_op | source)
XLA Modules:
  0.0 1309.9 jit_solution(1644639028979235806)
XLA Ops:
  7.2 4.1 stack.2
  11.2 19.1 %all-to-all-start = ((bf16[64,56,896]{2,1,0:T(8,128)(2,1)}), bf16[64,56,896]{2,1,0:T(8,128)(2,1)}, u32[]{:S(2)}, u32[]{:S(2)}) async-start(bf16[64,56,896]{2,1,0:T(8,128)(2,1)} %stack.2), calls=%async_computation | async-start | bytes 12845056 | tf_op jit(solution)/shard_map/all_to_all | solution.py:14
  30.7 1.3 fusion.23
  32.0 2.7 collective-permute-start
  34.7 1.3 collective-permute-start.1
  36.8 4.2 collective-permute-done.1
  40.9 1.7 pad_maximum_fusion
  42.9 1.4 slice_bitcast_fusion
  44.3 22.7 %while.10 = (s32[]{:T(128)}, bf16[4,96,896]{2,1,0:T(8,128)(2,1)}, bf16[4,192,896]{2,1,0:T(8,128)(2,1)}, pred[4,192]{1,0:T(4,128)(4,1)S(1)}, bf16[4,96,896]{2,1,0...) while((s32[]{:T(128)}, bf16[4,96,896]{2,1,0:T(8,128)(2,1)}, bf16[4,192,896]{2,1,0:T(8,128)(2,1)}, ...), condition=%wide.region_3.4_spmd, body=%wide.region_0.3_spmd.sunk | while | flops 67049856 | bytes 5857369 | solution.py:69
  44.3 1.0 constant_dynamic-slice_fusion.5
  46.0 1.4 fusion.44
  47.9 1.4 fusion.45
  49.3 0.7 bitcast_dynamic-update-slice_fusion.2
  50.0 1.0 constant_dynamic-slice_fusion.5
  51.7 1.4 fusion.44
  53.6 1.4 fusion.45
  55.0 0.7 bitcast_dynamic-update-slice_fusion.2
  55.7 1.0 constant_dynamic-slice_fusion.5
  57.4 1.4 fusion.44
  59.2 1.4 fusion.45
  60.7 0.7 bitcast_dynamic-update-slice_fusion.2
  61.3 1.0 constant_dynamic-slice_fusion.5
  63.1 1.4 fusion.44
  64.9 1.4 fusion.45
  66.3 0.7 bitcast_dynamic-update-slice_fusion.2
  67.1 317.4 %all-gather.2.cloned.1.call-done = bf16[2,2,96,3584]{3,2,1,0:T(8,128)(2,1)} async-done(((bf16[2,2,96,896]{3,2,1,0:T(8,128)(2,1)}), bf16[2,2,96,3584]{3,2,1,0:T(8,128)(2,1)}) %all-gather.2.cloned.1.call-update) | async-done | bytes 2752528 | tf_op jit(solution)/shard_map/all_gather | solution.py:94
  384.5 6.7 multiply_reduce_fusion
  391.3 9.1 psum.21
  400.8 250.4 %psum.23 = f32[896]{0:T(1024)S(1)} all-reduce(f32[896]{0:T(1024)S(1)} %fusion.27), channel_id=1, replica_groups=mesh['frames'=64,'mp'=4,'dp'=2] {'frames','dp'}, use_global_device_ids=true, to_apply=%region_9.10 | all-reduce | flops 896 | bytes 7168 | tf_op jit(solution)/shard_map/psum | solution.py:112
  651.3 0.8 multiply_convert_fusion
  652.1 1.2 multiply_multiply_fusion.1
  653.3 648.0 %psum.22 = f32[1]{0:T(128)} all-reduce(f32[1]{0:T(128)} %bitcast.12), channel_id=1, replica_groups=mesh['frames'=64,'mp'=4,'dp'=2] {'frames','mp'}, use_global_device_ids=true, to_apply=%region_8.9 | all-reduce | flops 1 | bytes 8 | tf_op jit(solution)/shard_map/psum | solution.py:107
  (55 shorter events, 6.1 us)
Async XLA Ops:
  11.2 19.2 %copy-start = (bf16[1,2,96,3,896]{4,2,3,1,0:T(8,128)(2,1)S(1)}, bf16[1,2,96,3,896]{4,2,3,1,0:T(8,128)(2,1)}, u32[]{:S(2)}) copy-start(bf16[1,2,96,3,896]{4,2,3,1,0:T(8,128)(2,1)} %param.7) | copy-start | bytes 3096580
  11.2 19.2 %copy-start.1 = (bf16[1,2,96,3,896]{4,2,3,1,0:T(8,128)(2,1)S(1)}, bf16[1,2,96,3,896]{4,2,3,1,0:T(8,128)(2,1)}, u32[]{:S(2)}) copy-start(bf16[1,2,96,3,896]{4,2,3,1,0:T(8,128)(2,1)} %param.8) | copy-start | bytes 3096580
  11.2 373.3 %all-to-all-start = ((bf16[64,56,896]{2,1,0:T(8,128)(2,1)}), bf16[64,56,896]{2,1,0:T(8,128)(2,1)}, u32[]{:S(2)}, u32[]{:S(2)}) async-start(bf16[64,56,896]{2,1,0:T(8,128)(2,1)} %stack.2), calls=%async_computation | async-start | bytes 12845056 | tf_op jit(solution)/shard_map/all_to_all | solution.py:14
  30.3 354.2 %all-gather.2.cloned.1.call-start = ((), (), s32[]{:S(2)}) async-start(), calls=%async_computation.1 | async-start | bytes 3440640 | tf_op jit(solution)/shard_map/all_gather | solution.py:94
  30.7 5.3 copy-start.3
  32.0 4.7 collective-permute-start
  34.7 6.2 collective-permute-start.1
  400.4 250.9 %copy-start.2 = (f32[896]{0:T(1024)S(1)}, f32[896]{0:T(1024)}, u32[]{:S(2)}) copy-start(f32[896]{0:T(1024)} %param.10) | copy-start | bytes 10756
Sparse Core Ops, SparseCore 0:
  67.2 317.3 all-gather.1
